TPU v7x, 32 devices: a whole 2x2x4 slice. The times are simulated.
32 devices in a mesh: section: 2 (over x), expert: 4 (over z), dp: 4 (over y, core).
Axes of the slice: x: 2, y: 2, z: 4, core: 2. Of those that a mesh axis runs over, the one named last changes fastest.
Arguments:
- fresh_tokens: bfloat16 [2, 1024, 4096], P(None, ('expert', 'dp')), may hold values from -60 to 60
- in_flight: bfloat16 [1024, 4096], P(('expert', 'dp')), may hold values from -60 to 60
- norm_weight: float32 [2, 4096], P('section'), may hold values from 0.1 to 1.9
- gate_up: bfloat16 [2, 16, 2, 4096, 768], P('section', 'expert', None, 'dp'), may hold values from -0.09375 to 0.09375
- down_proj: bfloat16 [2, 16, 768, 4096], P('section', 'expert', 'dp'), may hold values from -0.21875 to 0.21875
- first_moment: bfloat16 [2, 16, 768, 4096], P('section', 'expert', 'dp'), may hold values from -6 to 6
- second_moment: bfloat16 [2, 16, 768, 4096], P('section', 'expert', 'dp'), may hold values from 0.099609375 to 4
- route_ids: int32 [2, 2, 1024, 8], P('section', None, ('expert', 'dp')), may hold values from 0 to 15, all different within a row; in each aligned block of 64 rows (0 to 63, 64 to 127, ..., all dimensions but the last counted through in order) at most 36 rows name the same one
- route_probs: float32 [2, 2, 1024, 8], P('section', None, ('expert', 'dp')), may hold values from 0.05 to 1
- trade_flags: int32 [2, 4], replicated, may hold values from 0 to 1, as said below
Outputs:
- layer_out: bfloat16 [2, 2, 1024, 4096], P('section', None, ('expert', 'dp'))
- gate_up_moved: bfloat16 [2, 16, 2, 4096, 768], P('section', 'expert', None, 'dp')
- down_moved: bfloat16 [2, 16, 768, 4096], P('section', 'expert', 'dp')
- first_moved: bfloat16 [2, 16, 768, 4096], P('section', 'expert', 'dp')
- second_moved: bfloat16 [2, 16, 768, 4096], P('section', 'expert', 'dp')
Inputs may be any that keep to these rules, and one draw needn't show every extreme that they name: `route_ids`: in each aligned block of 64 rows (one device's tokens of one section and tick) the 8 experts of a token differ and no expert is chosen by more than 36 rows. `trade_flags`: at least one entry is 1 and at least one is 0.
All inputs are finite; a program needn't handle non-finite values.
Results may differ from a plain program's by a relative error of at most 0.0035.
Values may be sent and summed in bfloat16 or wider, within the bound.
No kernel may reach another device: no remote copies, remote signals or barrier semaphores. Data moves between devices by JAX's collectives and lax.ppermute only.
A program may use at most 256 MiB of HBM per device.

v0:
```python
import jax
import jax.numpy as jnp
from jax import lax
from jax.sharding import PartitionSpec as P

EXPERTS = 16
TOPK = 8
CAP = 36


def partner(value, axis, bit):
    return lax.ppermute(value, axis, [(i, i ^ 1 << bit) for i in range(lax.axis_size(axis))])


def shifted(block, axis, distance):
    devices = range(lax.axis_size(axis))
    route = [(i - distance, i) for i in devices if i - distance in devices]
    return lax.ppermute(block, axis, route)


def rms_normed(inputs, norm_gain):
    values = inputs.astype(jnp.float32)
    inverse_rms = lax.rsqrt(jnp.mean(values * values, axis=-1, keepdims=True) + 1e-06)
    return (values * inverse_rms * norm_gain).astype(jnp.bfloat16)


def per_device(
    fresh_tokens,
    in_flight,
    norm_weight,
    gate_up,
    down_proj,
    first_moment,
    second_moment,
    route_ids,
    route_probs,
    trade_flags,
):
    groups = lax.axis_size("expert")
    half_span = groups // 2
    top_bit = groups.bit_length() - 2
    own_rank = lax.axis_index("expert")
    section_index = lax.axis_index("section")
    experts_here = gate_up.shape[1]
    width = fresh_tokens.shape[2]
    own_flags = trade_flags[own_rank % half_span] == 1
    mask_five = own_flags[None, :, None, None, None]
    mask_four = own_flags[None, :, None, None]
    traded = partner((gate_up, down_proj, first_moment, second_moment), "expert", top_bit)
    gate_up_moved = jnp.where(mask_five, traded[0], gate_up)
    down_moved = jnp.where(mask_four, traded[1], down_proj)
    first_moved = jnp.where(mask_four, traded[2], first_moment)
    second_moved = jnp.where(mask_four, traded[3], second_moment)
    expert_ids = jnp.arange(EXPERTS, dtype=jnp.int32)
    home_block = expert_ids // experts_here
    home_slot = expert_ids % experts_here
    local_gate_up, local_down = (gate_up_moved, down_moved)
    expert_flags = trade_flags[home_block % half_span, home_slot]
    holder = jnp.where(expert_flags == 1, home_block ^ half_span, home_block)
    full_gate_up, full_down = (
        lax.all_gather(local_gate_up, "dp", axis=3, tiled=True),
        lax.all_gather(local_down, "dp", axis=2, tiled=True),
    )
    gate_weights = full_gate_up[0, :, 0]
    up_weights = full_gate_up[0, :, 1]
    down_weights = full_down[0]

    def expert_work(arrived):
        gate_part = jnp.einsum(
            "sicd,idf->sicf", arrived, gate_weights, preferred_element_type=jnp.float32
        )
        up_part = jnp.einsum(
            "sicd,idf->sicf", arrived, up_weights, preferred_element_type=jnp.float32
        )
        active = (jax.nn.silu(gate_part) * up_part).astype(jnp.bfloat16)
        result = jnp.einsum(
            "sicf,ifd->sicd", active, down_weights, preferred_element_type=jnp.float32
        ).astype(jnp.bfloat16)
        return lax.all_to_all(result, "expert", split_axis=0, concat_axis=0, tiled=True)

    def layer(inputs, layer_ids, layer_probs):
        normed = rms_normed(inputs, norm_weight[0])
        mix_weight = layer_probs / jnp.sum(layer_probs, axis=-1, keepdims=True)
        flat_ids = layer_ids.reshape(-1)
        one_hot = (flat_ids[:, None] == expert_ids[None, :]).astype(jnp.int32)
        slot_index = jnp.sum((jnp.cumsum(one_hot, axis=0) - 1) * one_hot, axis=1)
        target = holder[flat_ids]
        position = (target * experts_here + flat_ids % experts_here) * CAP + slot_index
        token_rows = jnp.arange(flat_ids.shape[0], dtype=jnp.int32) // TOPK
        outgoing = jnp.zeros((groups * experts_here * CAP, width), jnp.bfloat16)
        outgoing = outgoing.at[position].set(normed[token_rows])
        outgoing = outgoing.reshape(groups, experts_here, CAP, width)
        returned = expert_work(
            lax.all_to_all(outgoing, "expert", split_axis=0, concat_axis=0, tiled=True)
        )
        rows_back = returned.reshape(-1, width)[position].astype(jnp.float32)
        combined = jnp.sum(mix_weight[:, :, None] * rows_back.reshape(-1, TOPK, width), axis=1)
        return (inputs.astype(jnp.float32) + combined).astype(jnp.bfloat16)

    first_input = jnp.where(section_index == 0, fresh_tokens[0], in_flight)
    tick_zero = layer(first_input, route_ids[0, 0], route_probs[0, 0])
    arrived = shifted(tick_zero, "section", 1)
    second_input = jnp.where(section_index == 0, fresh_tokens[1], arrived)
    tick_one = layer(second_input, route_ids[0, 1], route_probs[0, 1])
    layer_out = jnp.stack([tick_zero, tick_one])[None]
    return (layer_out, gate_up_moved, down_moved, first_moved, second_moved)


def solution(mesh):
    return jax.shard_map(
        per_device,
        mesh=mesh,
        in_specs=(
            P(None, ("expert", "dp"), None),
            P(("expert", "dp"), None),
            P("section", None),
            P("section", "expert", None, "dp", None),
            P("section", "expert", "dp", None),
            P("section", "expert", "dp", None),
            P("section", "expert", "dp", None),
            P("section", None, ("expert", "dp"), None),
            P("section", None, ("expert", "dp"), None),
            P(),
        ),
        out_specs=(
            P("section", None, ("expert", "dp"), None),
            P("section", "expert", None, "dp", None),
            P("section", "expert", "dp", None),
            P("section", "expert", "dp", None),
            P("section", "expert", "dp", None),
        ),
        check_vma=False,
    )
```

profile of v0, /device:TPU:0, one launch (start us, length us, event | category | flops | bytes accessed | tf_op | source)
XLA Modules:
  0.0 2102.6 jit_solution(1615895428256260251)
XLA Ops:
  7.2 10.6 copy.38
  17.8 4.0 collective-permute-start.1
  21.8 540.3 %collective-permute-done.1 = bf16[1,4,2,1024,768]{4,3,1,2,0:T(8,128)(2,1)} collective-permute-done((bf16[1,4,2,1024,768]{4,3,1,2,0:T(8,128)(2,1)}, bf16[1,4,2,1024,768]{4,3,1,2,0:T(8,128)(2,1)}, u32[]{:S(2)}, u32[]{:S(2)}) %collective-permute-start.1) | collective-permute-done | bytes 12582944 | tf_op jit(solution)/shard_map/ppermute | solution.py:12
  562.1 13.5 broadcast_select_fusion
  575.8 2.9 collective-permute-start.3
  578.8 541.0 %collective-permute-done = bf16[1,4,192,4096]{3,2,1,0:T(8,128)(2,1)S(1)} collective-permute-done((bf16[1,4,192,4096]{3,2,1,0:T(8,128)(2,1)}, bf16[1,4,192,4096]{3,2,1,0:T(8,128)(2,1)S(1)}, u32[]{:S(2)}, u32[]{:S(2)}) %collective-permute-start) | collective-permute-done | bytes 6291488 | tf_op jit(solution)/shard_map/ppermute | solution.py:12
  1119.8 134.8 %collective-permute-done.3 = bf16[1,4,192,4096]{3,2,1,0:T(8,128)(2,1)S(1)} collective-permute-done((bf16[1,4,192,4096]{3,2,1,0:T(8,128)(2,1)}, bf16[1,4,192,4096]{3,2,1,0:T(8,128)(2,1)S(1)}, u32[]{:S(2)}, u32[]{:S(2)}) %collective-permute-start.3) | collective-permute-done | bytes 6291488 | tf_op jit(solution)/shard_map/ppermute | solution.py:12
  1254.6 133.2 %collective-permute-done.4 = bf16[1,4,192,4096]{3,2,1,0:T(8,128)(2,1)} collective-permute-done((bf16[1,4,192,4096]{3,2,1,0:T(8,128)(2,1)}, bf16[1,4,192,4096]{3,2,1,0:T(8,128)(2,1)}, u32[]{:S(2)}, u32[]{:S(2)}) %collective-permute-start.4) | collective-permute-done | bytes 6291488 | tf_op jit(solution)/shard_map/ppermute | solution.py:12
  1387.8 16.7 broadcast_select_fusion.1
  1404.5 0.6 copy-done.13
  1405.3 0.1 reshape_squeeze.6
  1405.4 0.1 eq.87
  1405.6 0.7 gather_fusion
  1406.2 0.1 copy.50
  1406.3 0.1 reshape_squeeze.7
  1406.4 1.2 reduce-window.14
  1407.6 0.2 slice_reduce_fusion.1
  1407.9 0.7 fusion.71
  1408.6 4.3 compare_select_fusion.9
  1413.0 0.1 fusion.56
  1413.1 0.3 fusion.44
  1413.4 5.5 select_multiply_fusion.1
  1419.0 0.2 fusion.46
  1419.2 21.4 %scatter_custom_fusion = bf16[576,4096]{1,0:T(8,128)(2,1)} fusion(s32[512]{0:T(512)S(1)} %bitcast.174, bf16[64,4096]{1,0:T(8,128)(2,1)S(1)} %fusion.46, s32[1024]{0:T(1024)S(1)} %pad_clamp_fusion.2, bf16[]{:T(256)} %constant.115.clone.1), kind=kCustom, calls=%fused_computation.35 | custom fusion | bytes 4718594 | tf_op jit(solution)/shard_map/scatter | solution.py:91
  1440.6 7.2 reshape.499
  1447.8 6.2 copy.44
  1454.0 107.1 %all_to_all.20 = bf16[4,4,36,4096]{3,1,2,0:T(4,128)(2,1)} all-to-all(bf16[4,4,36,4096]{3,1,2,0:T(4,128)(2,1)S(1)} %copy.44), channel_id=1, replica_groups=mesh['section'=2,'expert'=4,'dp'=4] {'expert'}, dimensions={0} | all-to-all | bytes 9437184 | tf_op jit(solution)/shard_map/all_to_all | solution.py:94
  1561.1 15.4 fusion.5
  1576.5 13.1 fusion.36
  1589.6 13.0 fusion.19
  1602.6 8.4 copy.47
  1611.0 5.3 all-to-all-start.1
  1616.6 1.2 reduce-window.16
  1617.8 0.2 slice_reduce_fusion
  1618.0 0.1 fusion.54
  1618.1 101.7 %all-to-all-done.1 = bf16[4,4,36,4096]{3,1,2,0:T(4,128)(2,1)} async-done(((bf16[4,4,36,4096]{3,1,2,0:T(4,128)(2,1)}), bf16[4,4,36,4096]{3,1,2,0:T(4,128)(2,1)}, u32[]{:S(2)}, u32[]{:S(2)}) %all-to-all-start.1) | async-done | bytes 4718624 | tf_op jit(solution)/shard_map/all_to_all | solution.py:79
  1719.8 7.3 copy.48
  1727.1 7.3 reshape.500
  1734.4 11.5 gather_fusion.1
  1746.0 5.8 fusion.9
  1751.8 0.1 fusion.47
  1751.9 3.7 collective-permute-start.2
  1755.6 5.5 select_multiply_fusion
  1761.1 4.3 collective-permute-done.2
  1765.4 0.3 fusion.48
  1765.7 0.8 copy-done.4
  1766.5 0.2 fusion.50
  1766.7 21.3 %scatter_custom_fusion.1 = bf16[576,4096]{1,0:T(8,128)(2,1)} fusion(s32[512]{0:T(512)S(1)} %bitcast.176, bf16[64,4096]{1,0:T(8,128)(2,1)S(1)} %fusion.50, s32[1024]{0:T(1024)S(1)} %pad_clamp_fusion.2, bf16[]{:T(256)} %constant.115.clone.1), kind=kCustom, calls=%fused_computation.33 | custom fusion | bytes 4718594 | tf_op jit(solution)/shard_map/scatter | solution.py:91
  1788.0 7.2 reshape.502
  1795.2 6.2 copy.54
  1801.4 105.8 %all_to_all.21 = bf16[4,4,36,4096]{3,1,2,0:T(4,128)(2,1)S(1)} all-to-all(bf16[4,4,36,4096]{3,1,2,0:T(4,128)(2,1)S(1)} %copy.54), channel_id=1, replica_groups=mesh['section'=2,'expert'=4,'dp'=4] {'expert'}, dimensions={0} | all-to-all | bytes 9437184 | tf_op jit(solution)/shard_map/all_to_all | solution.py:94
  1907.1 12.3 fusion.4
  1919.4 13.1 fusion.32
  1932.5 13.0 fusion.16
  1945.5 8.3 copy.57
  1953.8 5.2 all-to-all-start.3
  1959.1 10.6 copy.59
  1969.7 92.6 %all-to-all-done.3 = bf16[4,4,36,4096]{3,1,2,0:T(4,128)(2,1)} async-done(((bf16[4,4,36,4096]{3,1,2,0:T(4,128)(2,1)}), bf16[4,4,36,4096]{3,1,2,0:T(4,128)(2,1)}, u32[]{:S(2)}, u32[]{:S(2)}) %all-to-all-start.3) | async-done | bytes 4718624 | tf_op jit(solution)/shard_map/all_to_all | solution.py:79
  2062.3 7.3 copy.58
  2069.6 7.2 reshape.503
  2076.9 11.5 gather_fusion.2
  2088.4 5.7 fusion.8
  2094.1 0.1 fusion.52
  2094.2 1.1 maximum_bitcast_fusion
  (62 shorter events, 1.2 us)
Async XLA Ops:
  7.2 14.7 copy-start
  7.2 1553.9 %all-gather.5.cloned.1.call-start = ((), (), s32[]{:S(2)}) async-start(), calls=%async_computation.5 | async-start | bytes 62914560 | tf_op jit(solution)/shard_map/all_gather | solution.py:61
  17.8 544.3 %collective-permute-start.1 = (bf16[1,4,2,1024,768]{4,3,1,2,0:T(8,128)(2,1)}, bf16[1,4,2,1024,768]{4,3,1,2,0:T(8,128)(2,1)}, u32[]{:S(2)}, u32[]{:S(2)}) collective-permute-start(bf16[1,4,2,1024,768]{4,3,1,2,0:T(8,128)(2,1)} %copy.38), channel_id=1, source_target_pairs={{0,8},{4,12},{8,0},{12,4},{1,9},{5,13},{9,1},{13,5},{2,10},{6,14},... | collective-permute-start | bytes 37748744 | tf_op jit(solution)/shard_map/ppermute | solution.py:12
  575.7 1013.9 %all-gather.3.cloned.1.call-start = ((), (), s32[]{:S(2)}) async-start(), calls=%async_computation.4 | async-start | bytes 31457280 | tf_op jit(solution)/shard_map/all_gather | solution.py:62
  575.7 544.1 %collective-permute-start = (bf16[1,4,192,4096]{3,2,1,0:T(8,128)(2,1)}, bf16[1,4,192,4096]{3,2,1,0:T(8,128)(2,1)S(1)}, u32[]{:S(2)}, u32[]{:S(2)}) collective-permute-start(bf16[1,4,192,4096]{3,2,1,0:T(8,128)(2,1)} %param.14), channel_id=1, source_target_pairs={{0,8},{4,12},{8,0},{12,4},{1,9},{5,13},{9,1},{13,5},{2,10},{6,14},... | collective-permute-start | bytes 18874376 | tf_op jit(solution)/shard_map/ppermute | solution.py:12
  575.8 678.8 %collective-permute-start.3 = (bf16[1,4,192,4096]{3,2,1,0:T(8,128)(2,1)}, bf16[1,4,192,4096]{3,2,1,0:T(8,128)(2,1)S(1)}, u32[]{:S(2)}, u32[]{:S(2)}) collective-permute-start(bf16[1,4,192,4096]{3,2,1,0:T(8,128)(2,1)} %param.15), channel_id=1, source_target_pairs={{0,8},{4,12},{8,0},{12,4},{1,9},{5,13},{9,1},{13,5},{2,10},{6,14},... | collective-permute-start | bytes 18874376 | tf_op jit(solution)/shard_map/ppermute | solution.py:12
  578.7 809.1 %collective-permute-start.4 = (bf16[1,4,192,4096]{3,2,1,0:T(8,128)(2,1)}, bf16[1,4,192,4096]{3,2,1,0:T(8,128)(2,1)}, u32[]{:S(2)}, u32[]{:S(2)}) collective-permute-start(bf16[1,4,192,4096]{3,2,1,0:T(8,128)(2,1)} %param.16), channel_id=1, source_target_pairs={{0,8},{4,12},{8,0},{12,4},{1,9},{5,13},{9,1},{13,5},{2,10},{6,14},... | collective-permute-start | bytes 18874376 | tf_op jit(solution)/shard_map/ppermute | solution.py:12
  1404.5 0.7 copy-start.13
  1404.5 8.6 copy-start.8
  1404.5 8.6 copy-start.10
  1404.5 14.5 copy-start.11
  1413.4 5.6 copy-start.2
  1561.1 15.4 copy-start.1
  1611.0 5.5 copy-start.12
  1611.0 108.8 %all-to-all-start.1 = ((bf16[4,4,36,4096]{3,1,2,0:T(4,128)(2,1)}), bf16[4,4,36,4096]{3,1,2,0:T(4,128)(2,1)}, u32[]{:S(2)}, u32[]{:S(2)}) async-start(bf16[4,4,36,4096]{3,1,2,0:T(4,128)(2,1)} %copy.47), calls=%async_computation.1 | async-start | bytes 9437184 | tf_op jit(solution)/shard_map/all_to_all | solution.py:79
  1746.0 5.8 copy-start.3
  1746.0 19.5 copy-start.9
  1751.9 14.8 copy-start.6
  1751.9 13.6 collective-permute-start.2
  1765.7 0.8 copy-start.4
  1953.8 108.5 %all-to-all-start.3 = ((bf16[4,4,36,4096]{3,1,2,0:T(4,128)(2,1)}), bf16[4,4,36,4096]{3,1,2,0:T(4,128)(2,1)}, u32[]{:S(2)}, u32[]{:S(2)}) async-start(bf16[4,4,36,4096]{3,1,2,0:T(4,128)(2,1)} %copy.57), calls=%async_computation.3 | async-start | bytes 9437184 | tf_op jit(solution)/shard_map/all_to_all | solution.py:79
  2088.4 5.8 copy-start.5
  2088.4 5.9 copy-start.7
Sparse Core Ops, SparseCore 0:
  575.8 298.3 all-gather.4
  1404.7 152.3 all-gather.2
where the time goes:
time: 2110 us; the launch traced here: 2100 us
  waiting for transfers between devices  1550 us (73%)
  blocking collectives  213 us (10%)
  local copies, waits for them, and re-layouts  164 us (8%)
  matrix products  79.9 us (4%)
  other arithmetic  62 us (3%)
  starting transfers between devices  21.3 us (1%)
    ppermute x4, waiting for transfers between devices, partner(): lax.ppermute(value, axis, [(i, i ^ 1 << bit) for i in range(lax.axis_size...  1350 us
    all_to_all x2, blocking collectives, layer(): lax.all_to_all(outgoing, 'expert', split_axis=0, concat_axis=0, tiled=True)  213 us
    all_to_all x2, waiting for transfers between devices, expert_work(): lax.all_to_all(result, 'expert', split_axis=0, concat_axis=0, tiled=True)  194 us
    scatter x2, local copies, waits for them, and re-layouts, layer(): outgoing = outgoing.at[position].set(normed[token_rows])  42.7 us
  transfers between devices with their start and end apart: 9, of which 7 were waited for; matrix products, arithmetic and copies ran while one was open for 5% of the time, Pallas kernels for 0%

commit v1 on v0

v1 whole, which is shorter than its diff:
```python
import jax
import jax.numpy as jnp
from jax import lax
from jax.sharding import PartitionSpec as P

EXPERTS = 16
CAP = 36
COLUMN_PARTS = 4


def swap(value, axis, bit):
    return lax.ppermute(value, axis, [(i, i ^ (1 << bit)) for i in range(lax.axis_size(axis))])


def bits_of(axis):
    return lax.axis_size(axis).bit_length() - 1


def gather_relative(block, axis):
    held = block[None]
    for bit in reversed(range(bits_of(axis))):
        other = swap(held, axis, bit)
        held = jnp.stack([held, other], axis=1).reshape((-1,) + block.shape)
    return held


def scatter_relative(parts, axis):
    for bit in range(bits_of(axis)):
        paired = parts.reshape((parts.shape[0] // 2, 2) + parts.shape[1:])
        other = swap(paired[:, 1].astype(jnp.bfloat16), axis, bit)
        parts = paired[:, 0].astype(jnp.float32) + other.astype(jnp.float32)
    return parts[0]


def rms_normed(inputs, norm_gain):
    values = inputs.astype(jnp.float32)
    inverse_rms = lax.rsqrt(jnp.mean(values * values, axis=-1, keepdims=True) + 1e-06)
    return (values * inverse_rms * norm_gain).astype(jnp.bfloat16)


def exchange_slices(normed, dp_rank):
    ranks = lax.axis_size("dp")
    rows, width = normed.shape
    part = width // ranks
    columns = [
        lax.dynamic_slice_in_dim(normed, (dp_rank ^ r) * part, part, axis=1) for r in range(ranks)
    ]
    arrived = [columns[0]] + [
        lax.ppermute(columns[r], "dp", [(i, i ^ r) for i in range(ranks)]) for r in range(1, ranks)
    ]
    return jnp.concatenate(arrived, axis=0)


def route_tables(layer_ids, layer_probs):
    mix_weight = layer_probs / jnp.sum(layer_probs, axis=-1, keepdims=True)
    chosen = layer_ids[..., None] == jnp.arange(EXPERTS, dtype=jnp.int32)
    weights = jnp.sum(jnp.where(chosen, mix_weight[..., None], 0.0), axis=-2)
    member = jnp.any(chosen, axis=-2)
    rank = jnp.cumsum(member.astype(jnp.float32), axis=-2) - 1.0
    return weights, jnp.where(member, rank, -1.0)


def per_device(
    fresh_tokens,
    in_flight,
    norm_weight,
    gate_up,
    down_proj,
    first_moment,
    second_moment,
    route_ids,
    route_probs,
    trade_flags,
):
    groups = lax.axis_size("expert")
    dp_ranks = lax.axis_size("dp")
    half_span = groups // 2
    top_bit = bits_of("expert") - 1
    own_rank = lax.axis_index("expert")
    dp_rank = lax.axis_index("dp")
    section_index = lax.axis_index("section")
    experts_here = gate_up.shape[1]
    hidden = down_proj.shape[2]
    width = fresh_tokens.shape[2]
    block = fresh_tokens.shape[1]

    holdings = (gate_up, down_proj, first_moment, second_moment)
    counts = jnp.sum(trade_flags, axis=1)
    order = jnp.argsort(-trade_flags, axis=1, stable=True).astype(jnp.int32)
    own_pair = own_rank % half_span
    own_order = order[own_pair]
    own_count = counts[own_pair]

    def pair_route(pairs):
        return [(i, i ^ (1 << top_bit)) for i in range(groups) if i % half_span in pairs]

    def trade_round(moved, turn, pairs, beside_layers=False):
        slot = own_order[turn]
        active = turn < own_count
        if len(pairs) < half_span:
            active = jnp.logical_and(active, own_pair == pairs[0])
        sent = [lax.dynamic_slice_in_dim(array, slot, 1, axis=1) for array in holdings]
        if beside_layers:
            ranks = [[i, i + half_span] for i in range(half_span)]
            both = [lax.all_gather(array, "expert", axis_index_groups=ranks) for array in sent]
            other = 1 - own_rank // half_span
            arrived = [lax.dynamic_index_in_dim(array, other, 0, keepdims=False) for array in both]
        else:
            arrived = [lax.ppermute(array, "expert", pair_route(pairs)) for array in sent]
        return tuple(
            lax.dynamic_update_slice_in_dim(old, jnp.where(active, new, own), slot, axis=1)
            for old, new, own in zip(moved, arrived, sent)
        )

    moved = trade_round(holdings, jnp.int32(0), tuple(range(half_span)), beside_layers=True)

    def columns_for(relative):
        piece = lax.dynamic_slice_in_dim(gate_up[0], (dp_rank ^ relative) * hidden, hidden, axis=3)
        return jnp.concatenate([piece[:, 0], piece[:, 1]], axis=-1)

    pieces = [columns_for(r) for r in range(dp_ranks)]
    down_flat = down_proj[0].reshape(experts_here * hidden, width)

    weights, places = route_tables(route_ids[0], route_probs[0])
    table = jnp.stack([weights, places])
    gathered = lax.all_gather(table, ("expert", "dp"), axis=0, tiled=False)
    gathered = gathered.reshape((groups, dp_ranks) + table.shape)
    gathered = gathered[own_rank ^ jnp.arange(groups)][:, dp_rank ^ jnp.arange(dp_ranks)]
    mine = lax.dynamic_slice_in_dim(gathered, own_rank * experts_here, experts_here, axis=5)
    mix = mine[:, :, 0]
    place = mine[:, :, 1]
    group_rows = dp_ranks * CAP

    def layer(inputs, tick, after_columns):
        normed = rms_normed(inputs, norm_weight[0])
        tokens = gather_relative(exchange_slices(normed, dp_rank), "expert")
        tick_mix = mix[:, :, tick].reshape(groups, dp_ranks * block, experts_here)
        offset = ((dp_rank ^ jnp.arange(dp_ranks)) * CAP).astype(jnp.float32)[None, :, None, None]
        tick_place = place[:, :, tick]
        tick_place = jnp.where(tick_place >= 0, tick_place + offset, -1.0)
        tick_place = tick_place.reshape(groups, dp_ranks * block, experts_here)
        row_number = jnp.arange(group_rows, dtype=jnp.float32)[None, :, None]
        folded = []
        for expert in range(experts_here):
            pick = (tick_place[:, None, :, expert] == row_number).astype(jnp.bfloat16)
            rows = jnp.einsum(
                "grt,gtd->grd", pick, tokens, preferred_element_type=jnp.float32
            ).astype(jnp.bfloat16)
            rows = rows.reshape(groups * group_rows, -1)
            products = jnp.stack(
                [
                    jnp.dot(rows, piece[expert], preferred_element_type=jnp.float32)
                    for piece in pieces
                ]
            )
            total = scatter_relative(products, "dp")
            active = jax.nn.silu(total[:, :hidden]) * total[:, hidden:]
            active = active.astype(jnp.bfloat16).reshape(groups, group_rows, hidden)
            spread = jnp.einsum(
                "grt,grf->gtf", pick, active, preferred_element_type=jnp.float32
            )
            folded.append((spread * tick_mix[:, :, expert, None]).astype(jnp.bfloat16))
        folded = jnp.concatenate(folded, axis=-1).reshape(-1, experts_here * hidden)
        part = width // COLUMN_PARTS
        results, extras = [], []
        for index in range(COLUMN_PARTS):
            columns = slice(index * part, (index + 1) * part)
            product = jnp.dot(folded, down_flat[:, columns], preferred_element_type=jnp.float32)
            product = product.reshape(groups, dp_ranks, block, part)
            product = jnp.swapaxes(product, 0, 1)
            combined = scatter_relative(scatter_relative(product, "dp"), "expert")
            result = (inputs[:, columns].astype(jnp.float32) + combined).astype(jnp.bfloat16)
            results.append(result)
            extras.append(after_columns(result))
        return jnp.concatenate(results, axis=1), extras

    sections = lax.axis_size("section")
    onward = [(i, i + 1) for i in range(sections - 1)]
    first_input = jnp.where(section_index == 0, fresh_tokens[0], in_flight)
    tick_zero, arrived = layer(first_input, 0, lambda x: lax.ppermute(x, "section", onward))
    arrived = jnp.concatenate(arrived, axis=1)
    second_input = jnp.where(section_index == 0, fresh_tokens[1], arrived)
    tick_one, _ = layer(second_input, 1, lambda x: None)
    layer_out = jnp.stack([tick_zero, tick_one])[None]

    if experts_here > 1:
        moved, layer_out = lax.optimization_barrier((moved, layer_out))
        fewest = jnp.min(counts)
        everyone = tuple(range(half_span))
        moved = lax.fori_loop(
            1, fewest, lambda turn, held: trade_round(held, turn, everyone), moved
        )
        start = jnp.maximum(fewest, 1)
        for pair in range(half_span):
            moved = lax.fori_loop(
                start,
                counts[pair],
                lambda turn, held, pair=pair: trade_round(held, turn, (pair,)),
                moved,
            )
    return (layer_out,) + tuple(moved)


def solution(mesh):
    return jax.shard_map(
        per_device,
        mesh=mesh,
        in_specs=(
            P(None, ("expert", "dp"), None),
            P(("expert", "dp"), None),
            P("section", None),
            P("section", "expert", None, "dp", None),
            P("section", "expert", "dp", None),
            P("section", "expert", "dp", None),
            P("section", "expert", "dp", None),
            P("section", None, ("expert", "dp"), None),
            P("section", None, ("expert", "dp"), None),
            P(),
        ),
        out_specs=(
            P("section", None, ("expert", "dp"), None),
            P("section", "expert", None, "dp", None),
            P("section", "expert", "dp", None),
            P("section", "expert", "dp", None),
            P("section", "expert", "dp", None),
        ),
        check_vma=False,
    )
```

time: 2110 us -> 1450 us (0.69)
  waiting for transfers between devices: 1550 us -> 1030 us
  blocking collectives: 213 us -> 26.3 us
  starting transfers between devices: 21.3 us -> 81.8 us
    ppermute x5 -> x70, waiting for transfers between devices: 1350 us -> 1030 us  [the longest x8 633 us: trade_round(): lax.ppermute(array, 'expert', pair_route(pairs))]
    all_to_all x2 -> x0, blocking collectives: 213 us -> none  [layer(): lax.all_to_all(outgoing, 'expert', split_axis=0, concat_axis=0, tiled=True)]
    all_to_all x2 -> x0, waiting for transfers between devices: 194 us -> none  [expert_work(): lax.all_to_all(result, 'expert', split_axis=0, concat_axis=0, tiled=True)]
    ppermute x5 -> x70, starting transfers between devices: 10.8 us -> 81.7 us  [the longest x52 57.6 us: swap(): lax.ppermute(value, axis, [(i, i ^ 1 << bit) for i in range(lax.axis_size...]
    dynamic_slice x0 -> x20, local copies, waits for them, and re-layouts: none -> 56.1 us  [the longest x12 36.3 us: trade_round(): lax.dynamic_slice_in_dim(array, slot, 1, axis=1)]
    dynamic_update_slice x0 -> x12, other arithmetic: none -> 46.1 us  [trade_round(): lax.dynamic_update_slice_in_dim(old, jnp.where(active, new, own), slot, a...]
    unnamed x30 -> x148, local copies, waits for them, and re-layouts: 22.6 us -> 65.4 us
    scatter x2 -> x0, local copies, waits for them, and re-layouts: 42.7 us -> none  [layer(): outgoing = outgoing.at[position].set(normed[token_rows])]
  transfers between devices with their start and end apart: 9 -> 74, of which waited for: 7 -> 40; matrix products, arithmetic and copies ran while one was open for 5% -> 17% of each run, Pallas kernels for 0% -> 0%
where the time goes in v1:
time: 1450 us; the launch traced here: 1440 us
  waiting for transfers between devices  1030 us (71%)
  local copies, waits for them, and re-layouts  144 us (10%)
  starting transfers between devices  81.8 us (6%)
  other arithmetic  74.5 us (5%)
  matrix products  62.9 us (4%)
  blocking collectives  26.3 us (2%)
  between operations  19.6 us (1%)
    ppermute x8, waiting for transfers between devices, trade_round(): lax.ppermute(array, 'expert', pair_route(pairs))  633 us
    ppermute x52, waiting for transfers between devices, swap(): lax.ppermute(value, axis, [(i, i ^ 1 << bit) for i in range(lax.axis_size...  382 us
    unnamed x148, local copies, waits for them, and re-layouts  65.4 us
    ppermute x52, starting transfers between devices, swap(): lax.ppermute(value, axis, [(i, i ^ 1 << bit) for i in range(lax.axis_size...  57.6 us
    dynamic_update_slice x12, other arithmetic, trade_round(): lax.dynamic_update_slice_in_dim(old, jnp.where(active, new, own), slot, a...  46.1 us
    dot_general x32, matrix products, layer(): jnp.dot(rows, piece[expert], preferred_element_type=jnp.float32)  37.7 us
    dynamic_slice x12, local copies, waits for them, and re-layouts, trade_round(): lax.dynamic_slice_in_dim(array, slot, 1, axis=1)  36.3 us
  transfers between devices with their start and end apart: 74, of which 40 were waited for; matrix products, arithmetic and copies ran while one was open for 17% of the time, Pallas kernels for 0%

profile of v1, /device:TPU:0, one launch (start us, length us, event | category | flops | bytes accessed | tf_op | source)
XLA Modules:
  0.0 1444.0 jit_solution(420996344778418803)
XLA Ops:
  27.1 26.3 %all-gather.4 = f32[32,2,64,16]{2,3,1,0:T(8,128)S(1)} all-gather(f32[2,2,64,16]{2,3,1,0:T(8,128)S(1)} %pad_maximum_fusion.20), channel_id=6, replica_groups=mesh['section'=2,'expert'=4,'dp'=4] {'expert','dp'}, dimensions={0}, use_global_device_ids=true | all-gather | bytes 278528 | tf_op jit(solution)/shard_map/all_gather | solution.py:126
  55.1 16.5 %constant_dynamic-slice_fusion.17 = (bf16[1,4,2,1024,192]{4,3,2,1,0:T(8,128)(2,1)}, bf16[1,4,2,1024,192]{4,3,2,1,0:T(8,128)(2,1)}, bf16[1,4,2,1024,192]{4,3,2,1,0:T(8,128)(2,1)}, bf16[1,4,2,1024,192]{4,3,2,1,0:T(8,128)(2,1)}) fusion(bf16[1,4,2,1024,768]{4,3,2,1,0:T(8,128)(2,1)} %param.19, s32[]{:T(128)S(6)} %select_n.302, s32[]{:T(128)S(6)} %select_n.304, ...), kind=kLoop, calls=%fused_computation.510 | loop fusion | bytes 25165840 | tf_op jit(solution)/shard_map/dynamic_slice | solution.py:118
  71.6 6.1 copy.484
  83.8 24.3 %collective-permute-start.15 = (bf16[1,256,1024]{2,1,0:T(8,128)(2,1)}, bf16[1,256,1024]{2,1,0:T(8,128)(2,1)}, u32[]{:S(2)}, u32[]{:S(2)}) collective-permute-start(bf16[1,256,1024]{2,1,0:T(8,128)(2,1)} %get-tuple-element.518), channel_id=1, source_target_pairs={{0,8},{4,12},{8,0},{12,4},{1,9},{5,13},{9,1},{13,5},{2,10},{6,14},... | collective-permute-start | bytes 1572872 | tf_op jit(solution)/shard_map/ppermute | solution.py:12
  108.2 6.2 copy.482
  114.4 6.0 copy.480
  120.4 6.2 copy.478
  129.2 47.7 %collective-permute-done.15 = bf16[1,256,1024]{2,1,0:T(8,128)(2,1)} collective-permute-done((bf16[1,256,1024]{2,1,0:T(8,128)(2,1)}, bf16[1,256,1024]{2,1,0:T(8,128)(2,1)}, u32[]{:S(2)}, u32[]{:S(2)}) %collective-permute-start.15) | collective-permute-done | bytes 524320 | tf_op jit(solution)/shard_map/ppermute | solution.py:12
  180.8 3.2 copy-done.16
  184.5 38.4 %collective-permute-done.16 = bf16[2,256,1024]{2,1,0:T(8,128)(2,1)S(1)} collective-permute-done((bf16[2,256,1024]{2,1,0:T(8,128)(2,1)S(1)}, bf16[2,256,1024]{2,1,0:T(8,128)(2,1)S(1)}, u32[]{:S(2)}, u32[]{:S(2)}) %collective-permute-start.16) | collective-permute-done | bytes 1048608 | tf_op jit(solution)/shard_map/ppermute | solution.py:12
  236.8 12.9 convolution_bitcast_fusion.16
  258.1 8.1 collective-permute-done.18
  266.5 9.2 collective-permute-done.20
  275.8 9.4 collective-permute-done.22
  285.7 8.1 collective-permute-done.24
  299.4 3.8 fusion.47
  317.0 9.0 collective-permute-done.30
  326.2 11.0 collective-permute-done.34
  337.5 11.0 collective-permute-done.38
  348.7 10.0 collective-permute-done.26
  365.0 5.9 collective-permute-done.27
  371.1 3.7 constant_dynamic-slice_fusion.27
  386.0 3.4 collective-permute-start.41
  402.8 3.9 collective-permute-done.46
  410.2 11.1 copy.756
  421.4 3.2 copy.759
  424.6 6.6 copy.758
  438.3 3.6 fusion.33
  441.9 48.5 %collective-permute-done.48 = bf16[1,256,1024]{2,1,0:T(8,128)(2,1)} collective-permute-done((bf16[1,256,1024]{2,1,0:T(8,128)(2,1)}, bf16[1,256,1024]{2,1,0:T(8,128)(2,1)}, u32[]{:S(2)}, u32[]{:S(2)}) %collective-permute-start.48) | collective-permute-done | bytes 524320 | tf_op jit(solution)/shard_map/ppermute | solution.py:12
  491.7 3.6 fusion.34
  495.3 3.6 fusion.35
  499.0 69.1 %collective-permute-done.49 = bf16[2,256,1024]{2,1,0:T(8,128)(2,1)} collective-permute-done((bf16[2,256,1024]{2,1,0:T(8,128)(2,1)S(1)}, bf16[2,256,1024]{2,1,0:T(8,128)(2,1)}, u32[]{:S(2)}, u32[]{:S(2)}) %collective-permute-start.49) | collective-permute-done | bytes 1048608 | tf_op jit(solution)/shard_map/ppermute | solution.py:12
  598.2 8.1 collective-permute-done.51
  606.6 9.2 collective-permute-done.53
  615.8 9.4 collective-permute-done.55
  625.8 8.5 collective-permute-done.57
  640.3 3.8 fusion.46
  657.9 9.0 collective-permute-done.63
  667.1 11.0 collective-permute-done.67
  678.3 11.0 collective-permute-done.71
  689.6 10.0 collective-permute-done.59
  706.8 3.5 collective-permute-done.60
  711.4 5.2 fusion
  728.7 707.1 %while.52 = (s32[]{:T(128)}, bf16[1,4,2,1024,768]{4,3,2,1,0:T(8,128)(2,1)}, bf16[1,4,192,4096]{3,2,1,0:T(8,128)(2,1)}, bf16[1,4,192,4096]{3,2,1,0:T(8,128)(2,1)}...) while((s32[]{:T(128)}, ...), condition=%wide.region_10.11_spmd, body=%wide.region_9.10_spmd.sunk | while | flops 3932169 | bytes 70779304 | solution.py:190
  737.1 2.9 collective-permute-start.2
  740.1 3.8 constant_dynamic-slice_fusion.42
  746.7 2.9 collective-permute-start.3
  750.3 188.3 %collective-permute-done.1 = bf16[1,1,192,4096]{3,2,1,0:T(8,128)(2,1)} collective-permute-done((bf16[1,1,192,4096]{3,2,1,0:T(8,128)(2,1)}, bf16[1,1,192,4096]{3,2,1,0:T(8,128)(2,1)}, u32[]{:S(2)}, u32[]{:S(2)}) %collective-permute-start.1) | collective-permute-done | bytes 1572896 | tf_op jit(solution)/shard_map/while/body/ppermute | solution.py:109
  938.5 3.6 select_dynamic-update-slice_fusion.25
  942.1 30.1 %collective-permute-done.2 = bf16[1,1,192,4096]{3,2,1,0:T(8,128)(2,1)} collective-permute-done((bf16[1,1,192,4096]{3,2,1,0:T(8,128)(2,1)}, bf16[1,1,192,4096]{3,2,1,0:T(8,128)(2,1)}, u32[]{:S(2)}, u32[]{:S(2)}) %collective-permute-start.2) | collective-permute-done | bytes 1572896 | tf_op jit(solution)/shard_map/while/body/ppermute | solution.py:109
  972.2 3.6 select_dynamic-update-slice_fusion.26
  975.8 97.4 %collective-permute-done.3 = bf16[1,1,192,4096]{3,2,1,0:T(8,128)(2,1)} collective-permute-done((bf16[1,1,192,4096]{3,2,1,0:T(8,128)(2,1)}, bf16[1,1,192,4096]{3,2,1,0:T(8,128)(2,1)}, u32[]{:S(2)}, u32[]{:S(2)}) %collective-permute-start.3) | collective-permute-done | bytes 1572896 | tf_op jit(solution)/shard_map/while/body/ppermute | solution.py:109
  1073.3 3.6 select_dynamic-update-slice_fusion.27
  1076.8 4.3 select_dynamic-update-slice_fusion.24
  1089.6 2.9 collective-permute-start.2
  1092.5 3.8 constant_dynamic-slice_fusion.42
  1099.1 2.9 collective-permute-start.3
  1102.7 189.6 %collective-permute-done.1 = bf16[1,1,192,4096]{3,2,1,0:T(8,128)(2,1)} collective-permute-done((bf16[1,1,192,4096]{3,2,1,0:T(8,128)(2,1)}, bf16[1,1,192,4096]{3,2,1,0:T(8,128)(2,1)}, u32[]{:S(2)}, u32[]{:S(2)}) %collective-permute-start.1) | collective-permute-done | bytes 1572896 | tf_op jit(solution)/shard_map/while/body/ppermute | solution.py:109
  1292.3 3.6 select_dynamic-update-slice_fusion.25
  1295.9 30.1 %collective-permute-done.2 = bf16[1,1,192,4096]{3,2,1,0:T(8,128)(2,1)} collective-permute-done((bf16[1,1,192,4096]{3,2,1,0:T(8,128)(2,1)}, bf16[1,1,192,4096]{3,2,1,0:T(8,128)(2,1)}, u32[]{:S(2)}, u32[]{:S(2)}) %collective-permute-start.2) | collective-permute-done | bytes 1572896 | tf_op jit(solution)/shard_map/while/body/ppermute | solution.py:109
  1326.0 3.6 select_dynamic-update-slice_fusion.26
  1329.6 97.4 %collective-permute-done.3 = bf16[1,1,192,4096]{3,2,1,0:T(8,128)(2,1)} collective-permute-done((bf16[1,1,192,4096]{3,2,1,0:T(8,128)(2,1)}, bf16[1,1,192,4096]{3,2,1,0:T(8,128)(2,1)}, u32[]{:S(2)}, u32[]{:S(2)}) %collective-permute-start.3) | collective-permute-done | bytes 1572896 | tf_op jit(solution)/shard_map/while/body/ppermute | solution.py:109
  1427.0 3.6 select_dynamic-update-slice_fusion.27
  1430.6 4.3 select_dynamic-update-slice_fusion.24
  (507 shorter events, 206.8 us)
Async XLA Ops:
  7.2 431.1 %all-gather.16.cloned.1.call-start = ((), (), s32[]{:S(2)}) async-start(), calls=%async_computation.3 | async-start | bytes 4718592 | tf_op jit(solution)/shard_map/all_gather | solution.py:105
  15.3 476.4 %all-gather.14.cloned.1.call-start = ((), (), s32[]{:S(2)}) async-start(), calls=%async_computation.2 | async-start | bytes 4718592 | tf_op jit(solution)/shard_map/all_gather | solution.py:105
  18.2 477.1 %all-gather.12.cloned.1.call-start = ((), (), s32[]{:S(2)}) async-start(), calls=%async_computation.1 | async-start | bytes 4718592 | tf_op jit(solution)/shard_map/all_gather | solution.py:105
  20.4 61.4 %collective-permute-start.12 = (bf16[64,1024]{1,0:T(8,128)(2,1)}, bf16[64,1024]{1,0:T(8,128)(2,1)S(1)}, u32[]{:S(2)}, u32[]{:S(2)}) collective-permute-start(bf16[64,1024]{1,0:T(8,128)(2,1)} %get-tuple-element.522), channel_id=1, source_target_pairs={{0,1},{1,0},{2,3},{3,2},{4,5},{5,4},{6,7},{7,6},{8,9},{9,8},{10,11... | collective-permute-start | bytes 393224 | tf_op jit(solution)/shard_map/ppermute | solution.py:49
  20.8 60.9 %collective-permute-start.13 = (bf16[64,1024]{1,0:T(8,128)(2,1)}, bf16[64,1024]{1,0:T(8,128)(2,1)}, u32[]{:S(2)}, u32[]{:S(2)}) collective-permute-start(bf16[64,1024]{1,0:T(8,128)(2,1)} %get-tuple-element.521), channel_id=1, source_target_pairs={{0,2},{1,3},{2,0},{3,1},{4,6},{5,7},{6,4},{7,5},{8,10},{9,11},{10,... | collective-permute-start | bytes 393224 | tf_op jit(solution)/shard_map/ppermute | solution.py:49
  23.4 58.4 %collective-permute-start.14 = (bf16[64,1024]{1,0:T(8,128)(2,1)}, bf16[64,1024]{1,0:T(8,128)(2,1)}, u32[]{:S(2)}, u32[]{:S(2)}) collective-permute-start(bf16[64,1024]{1,0:T(8,128)(2,1)} %get-tuple-element.520), channel_id=1, source_target_pairs={{0,3},{1,2},{2,1},{3,0},{4,7},{5,6},{6,5},{7,4},{8,11},{9,10},{10,... | collective-permute-start | bytes 393224 | tf_op jit(solution)/shard_map/ppermute | solution.py:49
  26.4 685.0 %all-gather.10.cloned.1.call-start = ((), (), s32[]{:S(2)}) async-start(), calls=%async_computation | async-start | bytes 9437184 | tf_op jit(solution)/shard_map/all_gather | solution.py:105
  83.8 93.1 %collective-permute-start.15 = (bf16[1,256,1024]{2,1,0:T(8,128)(2,1)}, bf16[1,256,1024]{2,1,0:T(8,128)(2,1)}, u32[]{:S(2)}, u32[]{:S(2)}) collective-permute-start(bf16[1,256,1024]{2,1,0:T(8,128)(2,1)} %get-tuple-element.518), channel_id=1, source_target_pairs={{0,8},{4,12},{8,0},{12,4},{1,9},{5,13},{9,1},{13,5},{2,10},{6,14},... | collective-permute-start | bytes 1572872 | tf_op jit(solution)/shard_map/ppermute | solution.py:12
  178.2 44.8 %collective-permute-start.16 = (bf16[2,256,1024]{2,1,0:T(8,128)(2,1)S(1)}, bf16[2,256,1024]{2,1,0:T(8,128)(2,1)S(1)}, u32[]{:S(2)}, u32[]{:S(2)}) collective-permute-start(bf16[2,256,1024]{2,1,0:T(8,128)(2,1)S(1)} %get-tuple-element.502), channel_id=1, source_target_pairs={{0,4},{4,0},{8,12},{12,8},{1,5},{5,1},{9,13},{13,9},{2,6},{6,2},{1... | collective-permute-start | bytes 3145736 | tf_op jit(solution)/shard_map/ppermute | solution.py:12
  234.8 18.1 %collective-permute-start.17 = (bf16[2,576,384]{2,1,0:T(8,128)(2,1)S(1)}, bf16[2,576,384]{2,1,0:T(8,128)(2,1)S(1)}, u32[]{:S(2)}, u32[]{:S(2)}) collective-permute-start(bf16[2,576,384]{2,1,0:T(8,128)(2,1)S(1)} %fusion.74), channel_id=1, source_target_pairs={{0,1},{1,0},{2,3},{3,2},{4,5},{5,4},{6,7},{7,6},{8,9},{9,8},{10,11... | collective-permute-start | bytes 2654216 | tf_op jit(solution)/shard_map/ppermute | solution.py:12
  235.3 18.2 %collective-permute-start.19 = (bf16[2,576,384]{2,1,0:T(8,128)(2,1)S(1)}, bf16[2,576,384]{2,1,0:T(8,128)(2,1)S(1)}, u32[]{:S(2)}, u32[]{:S(2)}) collective-permute-start(bf16[2,576,384]{2,1,0:T(8,128)(2,1)S(1)} %fusion.75), channel_id=1, source_target_pairs={{0,1},{1,0},{2,3},{3,2},{4,5},{5,4},{6,7},{7,6},{8,9},{9,8},{10,11... | collective-permute-start | bytes 2654216 | tf_op jit(solution)/shard_map/ppermute | solution.py:12
  236.1 19.4 %collective-permute-start.21 = (bf16[2,576,384]{2,1,0:T(8,128)(2,1)S(1)}, bf16[2,576,384]{2,1,0:T(8,128)(2,1)S(1)}, u32[]{:S(2)}, u32[]{:S(2)}) collective-permute-start(bf16[2,576,384]{2,1,0:T(8,128)(2,1)S(1)} %fusion.76), channel_id=1, source_target_pairs={{0,1},{1,0},{2,3},{3,2},{4,5},{5,4},{6,7},{7,6},{8,9},{9,8},{10,11... | collective-permute-start | bytes 2654216 | tf_op jit(solution)/shard_map/ppermute | solution.py:12
  253.1 13.1 collective-permute-start.18
  253.7 21.9 %collective-permute-start.20 = (bf16[1,576,384]{2,1,0:T(8,128)(2,1)S(1)}, bf16[1,576,384]{2,1,0:T(8,128)(2,1)S(1)}, u32[]{:S(2)}, u32[]{:S(2)}) collective-permute-start(bf16[1,576,384]{2,1,0:T(8,128)(2,1)S(1)} %fusion.163), channel_id=1, source_target_pairs={{0,2},{1,3},{2,0},{3,1},{4,6},{5,7},{6,4},{7,5},{8,10},{9,11},{10,... | collective-permute-start | bytes 1327112 | tf_op jit(solution)/shard_map/ppermute | solution.py:12
  255.7 29.5 %collective-permute-start.22 = (bf16[1,576,384]{2,1,0:T(8,128)(2,1)S(1)}, bf16[1,576,384]{2,1,0:T(8,128)(2,1)S(1)}, u32[]{:S(2)}, u32[]{:S(2)}) collective-permute-start(bf16[1,576,384]{2,1,0:T(8,128)(2,1)S(1)} %fusion.164), channel_id=1, source_target_pairs={{0,2},{1,3},{2,0},{3,1},{4,6},{5,7},{6,4},{7,5},{8,10},{9,11},{10,... | collective-permute-start | bytes 1327112 | tf_op jit(solution)/shard_map/ppermute | solution.py:12
  256.3 37.5 %collective-permute-start.24 = (bf16[1,576,384]{2,1,0:T(8,128)(2,1)S(1)}, bf16[1,576,384]{2,1,0:T(8,128)(2,1)S(1)}, u32[]{:S(2)}, u32[]{:S(2)}) collective-permute-start(bf16[1,576,384]{2,1,0:T(8,128)(2,1)S(1)} %fusion.165), channel_id=1, source_target_pairs={{0,2},{1,3},{2,0},{3,1},{4,6},{5,7},{6,4},{7,5},{8,10},{9,11},{10,... | collective-permute-start | bytes 1327112 | tf_op jit(solution)/shard_map/ppermute | solution.py:12
  311.1 14.8 %collective-permute-start.30 = (bf16[1,4,64,1024]{3,2,1,0:T(8,128)(2,1)S(1)}, bf16[1,4,64,1024]{3,2,1,0:T(8,128)(2,1)S(1)}, u32[]{:S(2)}, u32[]{:S(2)}) collective-permute-start(bf16[1,4,64,1024]{3,2,1,0:T(8,128)(2,1)S(1)} %fusion.139), channel_id=1, source_target_pairs={{0,2},{1,3},{2,0},{3,1},{4,6},{5,7},{6,4},{7,5},{8,10},{9,11},{10,... | collective-permute-start | bytes 1572872 | tf_op jit(solution)/shard_map/ppermute | solution.py:12
  312.1 25.2 %collective-permute-start.34 = (bf16[1,4,64,1024]{3,2,1,0:T(8,128)(2,1)S(1)}, bf16[1,4,64,1024]{3,2,1,0:T(8,128)(2,1)S(1)}, u32[]{:S(2)}, u32[]{:S(2)}) collective-permute-start(bf16[1,4,64,1024]{3,2,1,0:T(8,128)(2,1)S(1)} %fusion.140), channel_id=1, source_target_pairs={{0,2},{1,3},{2,0},{3,1},{4,6},{5,7},{6,4},{7,5},{8,10},{9,11},{10,... | collective-permute-start | bytes 1572872 | tf_op jit(solution)/shard_map/ppermute | solution.py:12
  314.4 34.1 %collective-permute-start.38 = (bf16[1,4,64,1024]{3,2,1,0:T(8,128)(2,1)S(1)}, bf16[1,4,64,1024]{3,2,1,0:T(8,128)(2,1)S(1)}, u32[]{:S(2)}, u32[]{:S(2)}) collective-permute-start(bf16[1,4,64,1024]{3,2,1,0:T(8,128)(2,1)S(1)} %fusion.141), channel_id=1, source_target_pairs={{0,2},{1,3},{2,0},{3,1},{4,6},{5,7},{6,4},{7,5},{8,10},{9,11},{10,... | collective-permute-start | bytes 1572872 | tf_op jit(solution)/shard_map/ppermute | solution.py:12
  315.3 43.5 %collective-permute-start.26 = (bf16[1,4,64,1024]{3,2,1,0:T(8,128)(2,1)S(1)}, bf16[1,4,64,1024]{3,2,1,0:T(8,128)(2,1)S(1)}, u32[]{:S(2)}, u32[]{:S(2)}) collective-permute-start(bf16[1,4,64,1024]{3,2,1,0:T(8,128)(2,1)S(1)} %fusion.138), channel_id=1, source_target_pairs={{0,2},{1,3},{2,0},{3,1},{4,6},{5,7},{6,4},{7,5},{8,10},{9,11},{10,... | collective-permute-start | bytes 1572872 | tf_op jit(solution)/shard_map/ppermute | solution.py:12
  326.2 32.9 %collective-permute-start.31 = (bf16[2,64,1024]{2,1,0:T(8,128)(2,1)S(1)}, bf16[2,64,1024]{2,1,0:T(8,128)(2,1)S(1)}, u32[]{:S(2)}, u32[]{:S(2)}) collective-permute-start(bf16[2,64,1024]{2,1,0:T(8,128)(2,1)S(1)} %fusion.187), channel_id=1, source_target_pairs={{0,4},{4,0},{8,12},{12,8},{1,5},{5,1},{9,13},{13,9},{2,6},{6,2},{1... | collective-permute-start | bytes 786440 | tf_op jit(solution)/shard_map/ppermute | solution.py:12
  337.4 24.3 %collective-permute-start.35 = (bf16[2,64,1024]{2,1,0:T(8,128)(2,1)S(1)}, bf16[2,64,1024]{2,1,0:T(8,128)(2,1)S(1)}, u32[]{:S(2)}, u32[]{:S(2)}) collective-permute-start(bf16[2,64,1024]{2,1,0:T(8,128)(2,1)S(1)} %fusion.188), channel_id=1, source_target_pairs={{0,4},{4,0},{8,12},{12,8},{1,5},{5,1},{9,13},{13,9},{2,6},{6,2},{1... | collective-permute-start | bytes 786440 | tf_op jit(solution)/shard_map/ppermute | solution.py:12
  348.6 13.7 collective-permute-start.39
  359.0 12.0 collective-permute-start.27
  359.1 18.6 %collective-permute-start.32 = (bf16[1,64,1024]{2,1,0:T(8,128)(2,1)S(1)}, bf16[1,64,1024]{2,1,0:T(8,128)(2,1)S(1)}, u32[]{:S(2)}, u32[]{:S(2)}) collective-permute-start(bf16[1,64,1024]{2,1,0:T(8,128)(2,1)S(1)} %fusion.227), channel_id=1, source_target_pairs={{0,8},{4,12},{8,0},{12,4},{1,9},{5,13},{9,1},{13,5},{2,10},{6,14},... | collective-permute-start | bytes 393224 | tf_op jit(solution)/shard_map/ppermute | solution.py:12
  361.8 18.4 %collective-permute-start.36 = (bf16[1,64,1024]{2,1,0:T(8,128)(2,1)S(1)}, bf16[1,64,1024]{2,1,0:T(8,128)(2,1)S(1)}, u32[]{:S(2)}, u32[]{:S(2)}) collective-permute-start(bf16[1,64,1024]{2,1,0:T(8,128)(2,1)S(1)} %fusion.228), channel_id=1, source_target_pairs={{0,8},{4,12},{8,0},{12,4},{1,9},{5,13},{9,1},{13,5},{2,10},{6,14},... | collective-permute-start | bytes 393224 | tf_op jit(solution)/shard_map/ppermute | solution.py:12
  362.4 20.7 %collective-permute-start.40 = (bf16[1,64,1024]{2,1,0:T(8,128)(2,1)S(1)}, bf16[1,64,1024]{2,1,0:T(8,128)(2,1)S(1)}, u32[]{:S(2)}, u32[]{:S(2)}) collective-permute-start(bf16[1,64,1024]{2,1,0:T(8,128)(2,1)S(1)} %fusion.229), channel_id=1, source_target_pairs={{0,8},{4,12},{8,0},{12,4},{1,9},{5,13},{9,1},{13,5},{2,10},{6,14},... | collective-permute-start | bytes 393224 | tf_op jit(solution)/shard_map/ppermute | solution.py:12
  371.0 13.8 collective-permute-start.28
  386.0 7.9 collective-permute-start.41
  389.4 6.7 collective-permute-start.42
  390.7 7.6 collective-permute-start.43
  392.0 7.7 collective-permute-start.44
  400.4 6.4 collective-permute-start.46
  400.8 7.8 collective-permute-start.47
  409.6 80.8 %collective-permute-start.48 = (bf16[1,256,1024]{2,1,0:T(8,128)(2,1)}, bf16[1,256,1024]{2,1,0:T(8,128)(2,1)}, u32[]{:S(2)}, u32[]{:S(2)}) collective-permute-start(bf16[1,256,1024]{2,1,0:T(8,128)(2,1)} %get-tuple-element.508), channel_id=1, source_target_pairs={{0,8},{4,12},{8,0},{12,4},{1,9},{5,13},{9,1},{13,5},{2,10},{6,14},... | collective-permute-start | bytes 1572872 | tf_op jit(solution)/shard_map/ppermute | solution.py:12
  491.6 76.5 %collective-permute-start.49 = (bf16[2,256,1024]{2,1,0:T(8,128)(2,1)S(1)}, bf16[2,256,1024]{2,1,0:T(8,128)(2,1)}, u32[]{:S(2)}, u32[]{:S(2)}) collective-permute-start(bf16[2,256,1024]{2,1,0:T(8,128)(2,1)S(1)} %get-tuple-element.500), channel_id=1, source_target_pairs={{0,4},{4,0},{8,12},{12,8},{1,5},{5,1},{9,13},{13,9},{2,6},{6,2},{1... | collective-permute-start | bytes 3145736 | tf_op jit(solution)/shard_map/ppermute | solution.py:12
  589.1 5.7 collective-permute-start.52
  590.0 5.6 collective-permute-start.54
  593.2 13.0 collective-permute-start.51
  595.0 20.8 %collective-permute-start.53 = (bf16[1,576,384]{2,1,0:T(8,128)(2,1)S(1)}, bf16[1,576,384]{2,1,0:T(8,128)(2,1)S(1)}, u32[]{:S(2)}, u32[]{:S(2)}) collective-permute-start(bf16[1,576,384]{2,1,0:T(8,128)(2,1)S(1)} %fusion.167), channel_id=1, source_target_pairs={{0,2},{1,3},{2,0},{3,1},{4,6},{5,7},{6,4},{7,5},{8,10},{9,11},{10,... | collective-permute-start | bytes 1327112 | tf_op jit(solution)/shard_map/ppermute | solution.py:12
  595.8 29.4 %collective-permute-start.55 = (bf16[1,576,384]{2,1,0:T(8,128)(2,1)S(1)}, bf16[1,576,384]{2,1,0:T(8,128)(2,1)S(1)}, u32[]{:S(2)}, u32[]{:S(2)}) collective-permute-start(bf16[1,576,384]{2,1,0:T(8,128)(2,1)S(1)} %fusion.168), channel_id=1, source_target_pairs={{0,2},{1,3},{2,0},{3,1},{4,6},{5,7},{6,4},{7,5},{8,10},{9,11},{10,... | collective-permute-start | bytes 1327112 | tf_op jit(solution)/shard_map/ppermute | solution.py:12
  597.6 36.7 %collective-permute-start.57 = (bf16[1,576,384]{2,1,0:T(8,128)(2,1)S(1)}, bf16[1,576,384]{2,1,0:T(8,128)(2,1)S(1)}, u32[]{:S(2)}, u32[]{:S(2)}) collective-permute-start(bf16[1,576,384]{2,1,0:T(8,128)(2,1)S(1)} %fusion.169), channel_id=1, source_target_pairs={{0,2},{1,3},{2,0},{3,1},{4,6},{5,7},{6,4},{7,5},{8,10},{9,11},{10,... | collective-permute-start | bytes 1327112 | tf_op jit(solution)/shard_map/ppermute | solution.py:12
  648.1 5.4 collective-permute-start.66
  650.9 5.8 collective-permute-start.58
  652.0 14.8 %collective-permute-start.63 = (bf16[1,4,64,1024]{3,2,1,0:T(8,128)(2,1)S(1)}, bf16[1,4,64,1024]{3,2,1,0:T(8,128)(2,1)S(1)}, u32[]{:S(2)}, u32[]{:S(2)}) collective-permute-start(bf16[1,4,64,1024]{3,2,1,0:T(8,128)(2,1)S(1)} %fusion.143), channel_id=1, source_target_pairs={{0,2},{1,3},{2,0},{3,1},{4,6},{5,7},{6,4},{7,5},{8,10},{9,11},{10,... | collective-permute-start | bytes 1572872 | tf_op jit(solution)/shard_map/ppermute | solution.py:12
  654.0 24.0 %collective-permute-start.67 = (bf16[1,4,64,1024]{3,2,1,0:T(8,128)(2,1)S(1)}, bf16[1,4,64,1024]{3,2,1,0:T(8,128)(2,1)S(1)}, u32[]{:S(2)}, u32[]{:S(2)}) collective-permute-start(bf16[1,4,64,1024]{3,2,1,0:T(8,128)(2,1)S(1)} %fusion.144), channel_id=1, source_target_pairs={{0,2},{1,3},{2,0},{3,1},{4,6},{5,7},{6,4},{7,5},{8,10},{9,11},{10,... | collective-permute-start | bytes 1572872 | tf_op jit(solution)/shard_map/ppermute | solution.py:12
  655.2 34.1 %collective-permute-start.71 = (bf16[1,4,64,1024]{3,2,1,0:T(8,128)(2,1)S(1)}, bf16[1,4,64,1024]{3,2,1,0:T(8,128)(2,1)S(1)}, u32[]{:S(2)}, u32[]{:S(2)}) collective-permute-start(bf16[1,4,64,1024]{3,2,1,0:T(8,128)(2,1)S(1)} %fusion.145), channel_id=1, source_target_pairs={{0,2},{1,3},{2,0},{3,1},{4,6},{5,7},{6,4},{7,5},{8,10},{9,11},{10,... | collective-permute-start | bytes 1572872 | tf_op jit(solution)/shard_map/ppermute | solution.py:12
  657.3 42.4 %collective-permute-start.59 = (bf16[1,4,64,1024]{3,2,1,0:T(8,128)(2,1)S(1)}, bf16[1,4,64,1024]{3,2,1,0:T(8,128)(2,1)S(1)}, u32[]{:S(2)}, u32[]{:S(2)}) collective-permute-start(bf16[1,4,64,1024]{3,2,1,0:T(8,128)(2,1)S(1)} %fusion.142), channel_id=1, source_target_pairs={{0,2},{1,3},{2,0},{3,1},{4,6},{5,7},{6,4},{7,5},{8,10},{9,11},{10,... | collective-permute-start | bytes 1572872 | tf_op jit(solution)/shard_map/ppermute | solution.py:12
  667.0 32.9 %collective-permute-start.64 = (bf16[2,64,1024]{2,1,0:T(8,128)(2,1)S(1)}, bf16[2,64,1024]{2,1,0:T(8,128)(2,1)S(1)}, u32[]{:S(2)}, u32[]{:S(2)}) collective-permute-start(bf16[2,64,1024]{2,1,0:T(8,128)(2,1)S(1)} %fusion.191), channel_id=1, source_target_pairs={{0,4},{4,0},{8,12},{12,8},{1,5},{5,1},{9,13},{13,9},{2,6},{6,2},{1... | collective-permute-start | bytes 786440 | tf_op jit(solution)/shard_map/ppermute | solution.py:12
  678.3 24.1 %collective-permute-start.68 = (bf16[2,64,1024]{2,1,0:T(8,128)(2,1)S(1)}, bf16[2,64,1024]{2,1,0:T(8,128)(2,1)S(1)}, u32[]{:S(2)}, u32[]{:S(2)}) collective-permute-start(bf16[2,64,1024]{2,1,0:T(8,128)(2,1)S(1)} %fusion.192), channel_id=1, source_target_pairs={{0,4},{4,0},{8,12},{12,8},{1,5},{5,1},{9,13},{13,9},{2,6},{6,2},{1... | collective-permute-start | bytes 786440 | tf_op jit(solution)/shard_map/ppermute | solution.py:12
  689.5 14.8 %collective-permute-start.72 = (bf16[2,64,1024]{2,1,0:T(8,128)(2,1)S(1)}, bf16[2,64,1024]{2,1,0:T(8,128)(2,1)S(1)}, u32[]{:S(2)}, u32[]{:S(2)}) collective-permute-start(bf16[2,64,1024]{2,1,0:T(8,128)(2,1)S(1)} %fusion.193), channel_id=1, source_target_pairs={{0,4},{4,0},{8,12},{12,8},{1,5},{5,1},{9,13},{13,9},{2,6},{6,2},{1... | collective-permute-start | bytes 786440 | tf_op jit(solution)/shard_map/ppermute | solution.py:12
  699.8 10.4 collective-permute-start.60
  700.6 18.6 %collective-permute-start.65 = (bf16[1,64,1024]{2,1,0:T(8,128)(2,1)}, bf16[1,64,1024]{2,1,0:T(8,128)(2,1)S(1)}, u32[]{:S(2)}, u32[]{:S(2)}) collective-permute-start(bf16[1,64,1024]{2,1,0:T(8,128)(2,1)} %fusion.231), channel_id=1, source_target_pairs={{0,8},{4,12},{8,0},{12,4},{1,9},{5,13},{9,1},{13,5},{2,10},{6,14},... | collective-permute-start | bytes 393224 | tf_op jit(solution)/shard_map/ppermute | solution.py:12
  703.1 18.9 %collective-permute-start.69 = (bf16[1,64,1024]{2,1,0:T(8,128)(2,1)}, bf16[1,64,1024]{2,1,0:T(8,128)(2,1)S(1)}, u32[]{:S(2)}, u32[]{:S(2)}) collective-permute-start(bf16[1,64,1024]{2,1,0:T(8,128)(2,1)} %fusion.232), channel_id=1, source_target_pairs={{0,8},{4,12},{8,0},{12,4},{1,9},{5,13},{9,1},{13,5},{2,10},{6,14},... | collective-permute-start | bytes 393224 | tf_op jit(solution)/shard_map/ppermute | solution.py:12
  705.0 19.8 %collective-permute-start.73 = (bf16[1,64,1024]{2,1,0:T(8,128)(2,1)}, bf16[1,64,1024]{2,1,0:T(8,128)(2,1)S(1)}, u32[]{:S(2)}, u32[]{:S(2)}) collective-permute-start(bf16[1,64,1024]{2,1,0:T(8,128)(2,1)} %fusion.233), channel_id=1, source_target_pairs={{0,8},{4,12},{8,0},{12,4},{1,9},{5,13},{9,1},{13,5},{2,10},{6,14},... | collective-permute-start | bytes 393224 | tf_op jit(solution)/shard_map/ppermute | solution.py:12
  711.0 15.4 %collective-permute-start.61 = (bf16[1,64,1024]{2,1,0:T(8,128)(2,1)}, bf16[1,64,1024]{2,1,0:T(8,128)(2,1)}, u32[]{:S(2)}, u32[]{:S(2)}) collective-permute-start(bf16[1,64,1024]{2,1,0:T(8,128)(2,1)} %fusion.230), channel_id=1, source_target_pairs={{0,8},{4,12},{8,0},{12,4},{1,9},{5,13},{9,1},{13,5},{2,10},{6,14},... | collective-permute-start | bytes 393224 | tf_op jit(solution)/shard_map/ppermute | solution.py:12
  734.4 204.1 %collective-permute-start.1 = (bf16[1,1,192,4096]{3,2,1,0:T(8,128)(2,1)}, bf16[1,1,192,4096]{3,2,1,0:T(8,128)(2,1)}, u32[]{:S(2)}, u32[]{:S(2)}) collective-permute-start(bf16[1,1,192,4096]{3,2,1,0:T(8,128)(2,1)} %constant_dynamic-slice_fusion.43), channel_id=1, source_target_pairs={{0,8},{4,12},{8,0},{12,4},{1,9},{5,13},{9,1},{13,5},{2,10},{6,14},... | collective-permute-start | bytes 4718600 | tf_op jit(solution)/shard_map/while/body/ppermute | solution.py:109
  737.1 235.1 %collective-permute-start.2 = (bf16[1,1,192,4096]{3,2,1,0:T(8,128)(2,1)}, bf16[1,1,192,4096]{3,2,1,0:T(8,128)(2,1)}, u32[]{:S(2)}, u32[]{:S(2)}) collective-permute-start(bf16[1,1,192,4096]{3,2,1,0:T(8,128)(2,1)} %constant_dynamic-slice_fusion.44), channel_id=1, source_target_pairs={{0,8},{4,12},{8,0},{12,4},{1,9},{5,13},{9,1},{13,5},{2,10},{6,14},... | collective-permute-start | bytes 4718600 | tf_op jit(solution)/shard_map/while/body/ppermute | solution.py:109
  743.9 333.0 %collective-permute-start = (bf16[1,1,2,1024,768]{4,3,2,1,0:T(8,128)(2,1)}, bf16[1,1,2,1024,768]{4,3,2,1,0:T(8,128)(2,1)S(1)}, u32[]{:S(2)}, u32[]{:S(2)}) collective-permute-start(bf16[1,1,2,1024,768]{4,3,2,1,0:T(8,128)(2,1)} %constant_dynamic-slice_fusion.42), channel_id=1, source_target_pairs={{0,8},{4,12},{8,0},{12,4},{1,9},{5,13},{9,1},{13,5},{2,10},{6,14},... | collective-permute-start | bytes 9437192 | tf_op jit(solution)/shard_map/while/body/ppermute | solution.py:109
  746.7 326.6 %collective-permute-start.3 = (bf16[1,1,192,4096]{3,2,1,0:T(8,128)(2,1)}, bf16[1,1,192,4096]{3,2,1,0:T(8,128)(2,1)}, u32[]{:S(2)}, u32[]{:S(2)}) collective-permute-start(bf16[1,1,192,4096]{3,2,1,0:T(8,128)(2,1)} %constant_dynamic-slice_fusion.45), channel_id=1, source_target_pairs={{0,8},{4,12},{8,0},{12,4},{1,9},{5,13},{9,1},{13,5},{2,10},{6,14},... | collective-permute-start | bytes 4718600 | tf_op jit(solution)/shard_map/while/body/ppermute | solution.py:109
  1086.9 205.5 %collective-permute-start.1 = (bf16[1,1,192,4096]{3,2,1,0:T(8,128)(2,1)}, bf16[1,1,192,4096]{3,2,1,0:T(8,128)(2,1)}, u32[]{:S(2)}, u32[]{:S(2)}) collective-permute-start(bf16[1,1,192,4096]{3,2,1,0:T(8,128)(2,1)} %constant_dynamic-slice_fusion.43), channel_id=1, source_target_pairs={{0,8},{4,12},{8,0},{12,4},{1,9},{5,13},{9,1},{13,5},{2,10},{6,14},... | collective-permute-start | bytes 4718600 | tf_op jit(solution)/shard_map/while/body/ppermute | solution.py:109
  1089.6 236.4 %collective-permute-start.2 = (bf16[1,1,192,4096]{3,2,1,0:T(8,128)(2,1)}, bf16[1,1,192,4096]{3,2,1,0:T(8,128)(2,1)}, u32[]{:S(2)}, u32[]{:S(2)}) collective-permute-start(bf16[1,1,192,4096]{3,2,1,0:T(8,128)(2,1)} %constant_dynamic-slice_fusion.44), channel_id=1, source_target_pairs={{0,8},{4,12},{8,0},{12,4},{1,9},{5,13},{9,1},{13,5},{2,10},{6,14},... | collective-permute-start | bytes 4718600 | tf_op jit(solution)/shard_map/while/body/ppermute | solution.py:109
  1096.3 334.3 %collective-permute-start = (bf16[1,1,2,1024,768]{4,3,2,1,0:T(8,128)(2,1)}, bf16[1,1,2,1024,768]{4,3,2,1,0:T(8,128)(2,1)S(1)}, u32[]{:S(2)}, u32[]{:S(2)}) collective-permute-start(bf16[1,1,2,1024,768]{4,3,2,1,0:T(8,128)(2,1)} %constant_dynamic-slice_fusion.42), channel_id=1, source_target_pairs={{0,8},{4,12},{8,0},{12,4},{1,9},{5,13},{9,1},{13,5},{2,10},{6,14},... | collective-permute-start | bytes 9437192 | tf_op jit(solution)/shard_map/while/body/ppermute | solution.py:109
  1099.1 327.9 %collective-permute-start.3 = (bf16[1,1,192,4096]{3,2,1,0:T(8,128)(2,1)}, bf16[1,1,192,4096]{3,2,1,0:T(8,128)(2,1)}, u32[]{:S(2)}, u32[]{:S(2)}) collective-permute-start(bf16[1,1,192,4096]{3,2,1,0:T(8,128)(2,1)} %constant_dynamic-slice_fusion.45), channel_id=1, source_target_pairs={{0,8},{4,12},{8,0},{12,4},{1,9},{5,13},{9,1},{13,5},{2,10},{6,14},... | collective-permute-start | bytes 4718600 | tf_op jit(solution)/shard_map/while/body/ppermute | solution.py:109
  (72 other events, 1363.8 us)
Sparse Core Ops, SparseCore 0:
  15.4 84.3 all-gather.15
  101.3 98.4 all-gather.13
  201.3 79.1 all-gather.11
  374.9 170.8 all-gather.9
